TPU v7x, 32 devices: a whole 2x2x4 slice. The times are simulated.
32 devices in a mesh: groups: 2 (over y), rows: 4 (over z), shard: 4 (over x, core).
Axes of the slice: x: 2, y: 2, z: 4, core: 2. Of those that a mesh axis runs over, the one named last changes fastest.
Arguments:
- images: bfloat16 [8, 8, 128, 512], P(('groups', 'shard'), 'rows'), parts along dimension 0, may hold values from -6 to 6
- cotangent: bfloat16 [8, 8, 128, 512], P(('groups', 'shard'), 'rows'), parts along dimension 0, may hold values from -6 to 6
- weight_in: bfloat16 [2, 512, 512], P(None, 'shard'), may hold values from -0.25 to 0.25
- weight_group: bfloat16 [2, 144, 512], P(None, 'shard'), may hold values from -0.5 to 0.5
- weight_out: bfloat16 [2, 512, 512], P(None, 'shard'), may hold values from -0.25 to 0.25
Outputs:
- decoded: bfloat16 [8, 8, 128, 512], P(('groups', 'shard'), 'rows'), parts along dimension 0
- grad_images: bfloat16 [8, 8, 128, 512], P(('groups', 'shard'), 'rows'), parts along dimension 0
- grad_in: float32 [4, 512, 512], P('groups', 'shard'), parts along dimension 0
- grad_group: float32 [4, 144, 512], P('groups', 'shard'), parts along dimension 0
- grad_out: float32 [4, 512, 512], P('groups', 'shard'), parts along dimension 0
There are 2 independent parts, one for each index of `groups`. A program takes and returns all parts, laid end to end along the dimension named above; an argument that names none is the same for every part. Nothing has to cross between parts.
All inputs are finite; a program needn't handle non-finite values.
Results may differ from a plain program's by a relative error of at most 0.02.
Values may be sent and summed in bfloat16 or wider, within the bound.
A program may use at most 128 MiB of HBM per device.

v0:
```python
import math
import jax
import jax.numpy as jnp
from jax import lax
from jax.sharding import PartitionSpec as P

GW = 16


def extended_2(cells, sides, width):
    for axis, dim in sides:
        count = lax.axis_size(axis)
        ends = count - 1
        head = lax.slice_in_dim(cells, 0, width, axis=dim)
        tail = lax.slice_in_dim(cells, cells.shape[dim] - width, cells.shape[dim], axis=dim)
        cells = jnp.concatenate(
            [
                lax.ppermute(tail, axis, [(i, (i + 1) % count) for i in range(ends)]),
                cells,
                lax.ppermute(head, axis, [((i + 1) % count, i) for i in range(ends)]),
            ],
            axis=dim,
        )
    return cells


def silu_slope(preact):
    sigmoid_value = jax.nn.sigmoid(preact)
    return sigmoid_value * (1.0 + preact * (1.0 - sigmoid_value))


def block_kernel(full_group, hidden_width, group_width):
    sub_width = min(hidden_width, 128)
    sections = hidden_width // sub_width
    members = sub_width // group_width
    arranged = full_group.reshape(9, group_width, sections, members, group_width)
    arranged = arranged.transpose(0, 2, 3, 1, 4)
    identity = jnp.eye(members, dtype=full_group.dtype)
    expanded = arranged[:, :, :, :, None, :] * identity[None, None, :, None, :, None]
    return expanded.reshape(9, sections, sub_width, sub_width)


def grouped_taps(padded, kernel, out_rows, out_cols, flipped, pattern):
    summed = None
    for tap_index in range(9):
        row_step = tap_index // 3
        col_step = tap_index % 3
        if flipped:
            row_step = 2 - row_step
            col_step = 2 - col_step
        window = padded[:, row_step : row_step + out_rows, col_step : col_step + out_cols, :]
        window = window.reshape(-1, kernel.shape[1], kernel.shape[2])
        tap_term = jnp.einsum(
            pattern, window, kernel[tap_index], preferred_element_type=jnp.float32
        )
        summed = tap_term if summed is None else summed + tap_term
    return summed


def body(images, cotangent, weight_in, weight_group, weight_out):
    tile_count, height, across, channels = images.shape
    block_count = weight_in.shape[0]
    group_width = GW
    pixels = tile_count * height * across
    current = images.reshape(pixels, channels)
    stored = []
    for block_index in range(block_count):
        full_in, full_group, full_out = (
            lax.all_gather(weight_in[block_index], "shard", axis=0, tiled=True),
            lax.all_gather(weight_group[block_index], "shard", axis=0, tiled=True),
            lax.all_gather(weight_out[block_index], "shard", axis=0, tiled=True),
        )
        hidden_width = full_in.shape[1]
        kernel = block_kernel(full_group, hidden_width, group_width)
        pre_one = jnp.dot(current, full_in, preferred_element_type=jnp.float32)
        hidden_one = (
            jax.nn.silu(pre_one)
            .astype(jnp.bfloat16)
            .reshape(tile_count, height, across, hidden_width)
        )
        haloed = extended_2(hidden_one, (("rows", 1),), 1)
        padded_one = jnp.pad(haloed, ((0, 0), (0, 0), (1, 1), (0, 0)))
        pre_two = grouped_taps(padded_one, kernel, height, across, False, "psi,sio->pso").reshape(
            pixels, hidden_width
        )
        hidden_two = jax.nn.silu(pre_two).astype(jnp.bfloat16)
        pre_three = current.astype(jnp.float32) + jnp.dot(
            hidden_two, full_out, preferred_element_type=jnp.float32
        )
        kept_weights = None
        stored.append((current, pre_one, padded_one, pre_two, hidden_two, pre_three, kept_weights))
        current = jax.nn.silu(pre_three).astype(jnp.bfloat16)
    decoded = current.reshape(images.shape)
    grad_flow = cotangent.reshape(pixels, channels)
    shares = []
    for block_index in reversed(range(block_count)):
        flow_in, pre_one, padded_one, pre_two, hidden_two, pre_three, kept_weights = stored[
            block_index
        ]
        full_in, full_group, full_out = (
            lax.all_gather(weight_in[block_index], "shard", axis=0, tiled=True),
            lax.all_gather(weight_group[block_index], "shard", axis=0, tiled=True),
            lax.all_gather(weight_out[block_index], "shard", axis=0, tiled=True),
        )
        hidden_width = full_in.shape[1]
        kernel = block_kernel(full_group, hidden_width, group_width)
        sections = kernel.shape[1]
        sub_width = kernel.shape[2]
        members = sub_width // group_width
        slope_three = grad_flow.astype(jnp.float32) * silu_slope(pre_three)
        low_three = slope_three.astype(jnp.bfloat16)
        part_out = jnp.einsum(
            "pw,pc->wc", hidden_two, low_three, preferred_element_type=jnp.float32
        )
        slope_two = (
            jnp.einsum("pc,wc->pw", low_three, full_out, preferred_element_type=jnp.float32)
            * silu_slope(pre_two)
        ).astype(jnp.bfloat16)
        slope_sections = slope_two.reshape(pixels, sections, sub_width)
        tap_terms = []
        for tap_index in range(9):
            row_step = tap_index // 3
            col_step = tap_index % 3
            window = padded_one[:, row_step : row_step + height, col_step : col_step + across, :]
            window = window.reshape(pixels, sections, sub_width)
            blockwise = jnp.einsum(
                "psi,pso->sio", window, slope_sections, preferred_element_type=jnp.float32
            )
            blockwise = blockwise.reshape(sections, members, group_width, members, group_width)
            diagonal_part = jnp.diagonal(blockwise, axis1=1, axis2=3)
            tap_terms.append(diagonal_part.transpose(1, 0, 3, 2).reshape(group_width, hidden_width))
        part_group = jnp.stack(tap_terms).reshape(9 * group_width, hidden_width)
        slope_grid = slope_two.reshape(tile_count, height, across, hidden_width)
        padded_slope = jnp.pad(slope_grid, ((0, 0), (2, 2), (1, 1), (0, 0)))
        extended = grouped_taps(padded_slope, kernel, height + 2, across, True, "pso,sio->psi")
        extended = extended.reshape(tile_count, height + 2, across, hidden_width)
        edge_rows = jnp.concatenate([extended[:, :1], extended[:, -1:]], axis=1)
        borders = extended_2(edge_rows.astype(jnp.bfloat16), (("rows", 1),), 1).astype(
            edge_rows.dtype
        )
        back_one = extended[:, 1:-1]
        back_one = back_one.at[:, :1].add(borders[:, :1])
        back_one = back_one.at[:, -1:].add(borders[:, -1:])
        slope_one = (back_one.reshape(pixels, hidden_width) * silu_slope(pre_one)).astype(
            jnp.bfloat16
        )
        part_in = jnp.einsum("pc,pw->cw", flow_in, slope_one, preferred_element_type=jnp.float32)
        grad_flow = (
            slope_three
            + jnp.einsum("pw,cw->pc", slope_one, full_in, preferred_element_type=jnp.float32)
        ).astype(jnp.bfloat16)
        shares.append(
            (
                lax.psum_scatter(
                    part_in.astype(jnp.bfloat16), "shard", scatter_dimension=0, tiled=True
                ).astype(jnp.float32),
                lax.psum_scatter(
                    part_group.astype(jnp.bfloat16), "shard", scatter_dimension=0, tiled=True
                ).astype(jnp.float32),
                lax.psum_scatter(
                    part_out.astype(jnp.bfloat16), "shard", scatter_dimension=0, tiled=True
                ).astype(jnp.float32),
            )
        )
    shares = shares[::-1]
    totals = (
        lax.psum(jnp.stack([entry[0] for entry in shares]).astype(jnp.bfloat16), "rows").astype(
            jnp.float32
        ),
        lax.psum(jnp.stack([entry[1] for entry in shares]).astype(jnp.bfloat16), "rows").astype(
            jnp.float32
        ),
        lax.psum(jnp.stack([entry[2] for entry in shares]).astype(jnp.bfloat16), "rows").astype(
            jnp.float32
        ),
    )
    norm_factor = 1.0 / math.sqrt(pixels * lax.axis_size("rows") * lax.axis_size("shard"))
    grad_images = grad_flow.reshape(images.shape)
    return (
        decoded,
        grad_images,
        totals[0] * norm_factor,
        totals[1] * norm_factor,
        totals[2] * norm_factor,
    )


def solution(mesh):
    placed = (
        P(("groups", "shard"), "rows", None, None),
        P(("groups", "shard"), "rows", None, None),
        P(None, "shard", None),
        P(None, "shard", None),
        P(None, "shard", None),
    )
    return jax.shard_map(
        body,
        mesh=mesh,
        in_specs=placed,
        out_specs=(
            P(("groups", "shard"), "rows", None, None),
            P(("groups", "shard"), "rows", None, None),
            P("groups", "shard", None),
            P("groups", "shard", None),
            P("groups", "shard", None),
        ),
        check_vma=False,
    )
```

profile of v0, /device:TPU:0, one launch (start us, length us, event | category | flops | bytes accessed | tf_op | source)
XLA Modules:
  0.0 434.7 jit_solution(18209110213923368101)
XLA Ops:
  8.9 8.6 %all-gather.1 = bf16[1,512,512]{2,1,0:T(8,128)(2,1)S(1)} all-gather(bf16[1,128,512]{2,1,0:T(8,128)(2,1)S(1)} %get-tuple-element.137), channel_id=3, replica_groups=mesh['groups'=2,'rows'=4,'shard'=4] {'shard'}, dimensions={1}, use_global_device_ids=true | all-gather | bytes 655360 | tf_op jit(solution)/shard_map/all_gather | solution.py:69
  20.6 5.2 %collective-permute-start = (bf16[1,1,128,512]{3,2,1,0:T(8,128)(2,1)}, bf16[1,1,128,512]{3,2,1,0:T(8,128)(2,1)}, u32[]{:S(2)}, u32[]{:S(2)}) collective-permute-start(bf16[1,1,128,512]{3,2,1,0:T(8,128)(2,1)} %get-tuple-element.135), channel_id=1, source_target_pairs={{0,4},{4,8},{8,12},{1,5},{5,9},{9,13},{2,6},{6,10},{10,14},{3,7},{... | collective-permute-start | bytes 393224 | tf_op jit(solution)/shard_map/ppermute | solution.py:18
  27.5 5.9 %all-gather = bf16[1,144,512]{2,0,1:T(2,128)(2,1)S(1)} all-gather(bf16[1,36,512]{2,0,1:T(2,128)(2,1)S(1)} %get-tuple-element.141), channel_id=2, replica_groups=mesh['groups'=2,'rows'=4,'shard'=4] {'shard'}, dimensions={1}, use_global_device_ids=true | all-gather | bytes 184320 | tf_op jit(solution)/shard_map/all_gather | solution.py:70
  36.6 6.0 %all-gather.3 = bf16[1,144,512]{2,0,1:T(2,128)(2,1)S(1)} all-gather(bf16[1,36,512]{2,0,1:T(2,128)(2,1)S(1)} %get-tuple-element.142), channel_id=5, replica_groups=mesh['groups'=2,'rows'=4,'shard'=4] {'shard'}, dimensions={1}, use_global_device_ids=true | all-gather | bytes 184320 | tf_op jit(solution)/shard_map/all_gather | solution.py:70
  45.9 9.3 %all-gather.4 = bf16[1,512,512]{2,1,0:T(8,128)(2,1)} all-gather(bf16[1,128,512]{2,1,0:T(8,128)(2,1)} %get-tuple-element.138), channel_id=6, replica_groups=mesh['groups'=2,'rows'=4,'shard'=4] {'shard'}, dimensions={1}, use_global_device_ids=true | all-gather | bytes 655360 | tf_op jit(solution)/shard_map/all_gather | solution.py:69
  55.2 4.4 %broadcast_multiply_fusion.1 = (bf16[9,4,8,16,8,16]{3,2,5,4,1,0:T(8,128)(2,1)S(1)}, bf16[9,4,8,16,8,16]{3,2,5,4,1,0:T(8,128)(2,1)}) fusion(bf16[8,8]{0,1:T(8,128)(2,1)S(1)} %fusion.107, bf16[9,4,8,16,16]{3,2,4,1,0:T(8,128)(2,1)S(1)} %copy.227, bf16[9,4,8,16,16]{3,2,4,1,0:T(8,128)(2,1)S(1)} %copy.238), kind=kLoop, calls=%fused_computation.19 | loop fusion | flops 1179648 | bytes 2654336 | tf_op jit(solution)/shard_map/mul | solution.py:39
  59.6 9.0 %fusion.109 = (bf16[1,4,8,16,8,16]{3,2,5,4,1,0:T(8,128)(2,1)S(1)}, bf16[1,4,8,16,8,16]{3,2,5,4,1,0:T(8,128)(2,1)S(1)}, bf16[1,4,8,16,8,16]{3,2,5,4,1,0:T(8,128)(...) fusion(bf16[9,4,8,16,8,16]{3,2,5,4,1,0:T(8,128)(2,1)} %get-tupl, ...), kind=kLoop, calls=%fused_computation.285 | loop fusion | bytes 4718592 | tf_op jit(solution)/shard_map/slice | solution.py:54
  70.6 2.6 squeeze.99
  75.9 2.6 squeeze.101
  83.7 2.6 squeeze.104
  88.9 2.6 squeeze.106
  91.5 8.8 %all-gather.2 = bf16[1,512,512]{2,1,0:T(8,128)(2,1)} all-gather(bf16[1,128,512]{2,1,0:T(8,128)(2,1)} %get-tuple-element.139), channel_id=4, replica_groups=mesh['groups'=2,'rows'=4,'shard'=4] {'shard'}, dimensions={1}, use_global_device_ids=true | all-gather | bytes 655360 | tf_op jit(solution)/shard_map/all_gather | solution.py:71
  143.5 5.2 %collective-permute-start.2 = (bf16[1,1,128,512]{3,2,1,0:T(8,128)(2,1)}, bf16[1,1,128,512]{3,2,1,0:T(8,128)(2,1)}, u32[]{:S(2)}, u32[]{:S(2)}) collective-permute-start(bf16[1,1,128,512]{3,2,1,0:T(8,128)(2,1)} %get-tuple-element.131), channel_id=1, source_target_pairs={{0,4},{4,8},{8,12},{1,5},{5,9},{9,13},{2,6},{6,10},{10,14},{3,7},{... | collective-permute-start | bytes 393224 | tf_op jit(solution)/shard_map/ppermute | solution.py:18
  148.7 7.2 %all-gather.5 = bf16[1,512,512]{2,1,0:T(8,128)(2,1)} all-gather(bf16[1,128,512]{2,1,0:T(8,128)(2,1)S(1)} %copy-done.92), channel_id=7, replica_groups=mesh['groups'=2,'rows'=4,'shard'=4] {'shard'}, dimensions={1}, use_global_device_ids=true | all-gather | bytes 655360 | tf_op jit(solution)/shard_map/all_gather | solution.py:71
  155.9 2.6 squeeze.109
  168.9 2.8 squeeze.115
  186.2 2.7 convert_multiply_fusion
  223.7 5.2 %collective-permute-start.4 = (bf16[1,1,128,512]{3,2,1,0:T(8,128)(2,1)}, bf16[1,1,128,512]{3,2,1,0:T(8,128)(2,1)}, u32[]{:S(2)}, u32[]{:S(2)}) collective-permute-start(bf16[1,1,128,512]{3,2,1,0:T(8,128)(2,1)} %copy.401), channel_id=1, source_target_pairs={{0,4},{4,8},{8,12},{1,5},{5,9},{9,13},{2,6},{6,10},{10,14},{3,7},{... | collective-permute-start | bytes 393224 | tf_op jit(solution)/shard_map/ppermute | solution.py:18
  291.5 5.4 %collective-permute-start.6 = (bf16[1,1,128,512]{3,2,1,0:T(8,128)(2,1)}, bf16[1,1,128,512]{3,2,1,0:T(8,128)(2,1)}, u32[]{:S(2)}, u32[]{:S(2)}) collective-permute-start(bf16[1,1,128,512]{3,2,1,0:T(8,128)(2,1)} %copy.405), channel_id=1, source_target_pairs={{0,4},{4,8},{8,12},{1,5},{5,9},{9,13},{2,6},{6,10},{10,14},{3,7},{... | collective-permute-start | bytes 393224 | tf_op jit(solution)/shard_map/ppermute | solution.py:18
  330.3 8.6 %fusion.108 = (bf16[40,512]{1,0:T(8,128)(2,1)S(1)}, bf16[40,512]{1,0:T(8,128)(2,1)S(1)}) fusion(bf16[144,512]{1,0:T(8,128)(2,1)} %bitcast.72, bf16[144,512]{1,0:T(8,128)(2,1)S(1)} %bitcast.611), kind=kCustom, calls=%all-reduce-scatter.2 | all-reduce-scatter fusion | flops 163841 | bytes 377344
  340.3 3.7 collective-permute-start.8
  348.4 7.7 %reduce-scatter.21.cloned.1.call-done = bf16[128,512]{1,0:T(8,128)(2,1)} async-done(((bf16[512,512]{1,0:T(8,128)(2,1)}), bf16[128,512]{1,0:T(8,128)(2,1)}) %reduce-scatter.21.cloned.1.call-update) | async-done | bytes 131088
  357.9 23.0 %reduce-scatter.17.cloned.1.call-done = bf16[128,512]{1,0:T(8,128)(2,1)} async-done(((bf16[512,512]{1,0:T(8,128)(2,1)}), bf16[128,512]{1,0:T(8,128)(2,1)}) %reduce-scatter.17.cloned.1.call-update) | async-done | bytes 131088
  383.8 40.3 %all-reduce.12.cloned.1.call-done = (bf16[2,128,512]{1,2,0:T(8,128)(2,1)}, bf16[2,36,512]{2,1,0:T(8,128)(2,1)}, bf16[2,128,512]{1,2,0:T(8,128)(2,1)}) async-done(((bf16[2,128,512]{1,2,0:T(8,128)(2,1)}, bf16[2,36,512]{2,1,0:T(8,128)(2,1)}, bf16[2,128,512]{1,2,0:T(8,128)(2,1)}), (bf16[2,128,512]{1,2,0:T(8,128)(2,1)}, bf16[2,36,512]{2,1,0:T(8,128)(2,1)}, ...) | async-done | bytes 598032 | tf_op jit(solution)/shard_map/psum | solution.py:167
  (578 shorter events, 235.6 us)
Async XLA Ops:
  7.2 10.3 %copy-start.98 = (bf16[1,2,128,512]{3,2,1,0:T(8,128)(2,1)S(1)}, bf16[1,2,128,512]{3,2,1,0:T(8,128)(2,1)}, u32[]{:S(2)}) copy-start(bf16[1,2,128,512]{3,2,1,0:T(8,128)(2,1)} %param.13) | copy-start | bytes 786436
  7.2 339.2 %reduce-scatter.23.cloned.1.call-start = ((), (), s32[]{:S(2)}) async-start(), calls=%async_computation.7 | async-start | bytes 655360
  18.6 14.8 %copy-start = (bf16[256,512]{1,0:T(8,128)(2,1)}, bf16[256,512]{1,0:T(8,128)(2,1)S(1)}, u32[]{:S(2)}) copy-start(bf16[256,512]{1,0:T(8,128)(2,1)S(1)} %get-tuple-element.145) | copy-start | bytes 786436
  18.6 8.8 %copy-start.93 = (bf16[2,36,512]{2,0,1:T(2,128)(2,1)S(1)}, bf16[2,36,512]{2,0,1:T(2,128)(2,1)}, u32[]{:S(2)}) copy-start(bf16[2,36,512]{2,0,1:T(2,128)(2,1)} %param.16) | copy-start | bytes 221188
  19.3 81.0 %collective-permute-start.1 = (bf16[1,1,128,512]{3,2,1,0:T(8,128)(2,1)}, bf16[1,1,128,512]{3,2,1,0:T(8,128)(2,1)}, u32[]{:S(2)}, u32[]{:S(2)}) collective-permute-start(bf16[1,1,128,512]{3,2,1,0:T(8,128)(2,1)} %get-tuple-element.136), channel_id=1, source_target_pairs={{4,0},{8,4},{12,8},{5,1},{9,5},{13,9},{6,2},{10,6},{14,10},{7,3},{... | collective-permute-start | bytes 393224 | tf_op jit(solution)/shard_map/ppermute | solution.py:20
  20.6 79.7 %collective-permute-start = (bf16[1,1,128,512]{3,2,1,0:T(8,128)(2,1)}, bf16[1,1,128,512]{3,2,1,0:T(8,128)(2,1)}, u32[]{:S(2)}, u32[]{:S(2)}) collective-permute-start(bf16[1,1,128,512]{3,2,1,0:T(8,128)(2,1)} %get-tuple-element.135), channel_id=1, source_target_pairs={{0,4},{4,8},{8,12},{1,5},{5,9},{9,13},{2,6},{6,10},{10,14},{3,7},{... | collective-permute-start | bytes 393224 | tf_op jit(solution)/shard_map/ppermute | solution.py:18
  88.9 11.5 %copy-start.1 = (bf16[256,512]{1,0:T(8,128)(2,1)S(1)}, bf16[256,512]{1,0:T(8,128)(2,1)}, u32[]{:S(2)}) copy-start(bf16[256,512]{1,0:T(8,128)(2,1)} %copy-done) | copy-start | bytes 786436
  142.2 33.0 %collective-permute-start.3 = (bf16[1,1,128,512]{3,2,1,0:T(8,128)(2,1)}, bf16[1,1,128,512]{3,2,1,0:T(8,128)(2,1)}, u32[]{:S(2)}, u32[]{:S(2)}) collective-permute-start(bf16[1,1,128,512]{3,2,1,0:T(8,128)(2,1)} %get-tuple-element.132), channel_id=1, source_target_pairs={{4,0},{8,4},{12,8},{5,1},{9,5},{13,9},{6,2},{10,6},{14,10},{7,3},{... | collective-permute-start | bytes 393224 | tf_op jit(solution)/shard_map/ppermute | solution.py:20
  143.5 31.8 %collective-permute-start.2 = (bf16[1,1,128,512]{3,2,1,0:T(8,128)(2,1)}, bf16[1,1,128,512]{3,2,1,0:T(8,128)(2,1)}, u32[]{:S(2)}, u32[]{:S(2)}) collective-permute-start(bf16[1,1,128,512]{3,2,1,0:T(8,128)(2,1)} %get-tuple-element.131), channel_id=1, source_target_pairs={{0,4},{4,8},{8,12},{1,5},{5,9},{9,13},{2,6},{6,10},{10,14},{3,7},{... | collective-permute-start | bytes 393224 | tf_op jit(solution)/shard_map/ppermute | solution.py:18
  173.7 10.5 %copy-start.48 = (bf16[4,128,128]{1,2,0:T(8,128)(2,1)}, bf16[4,128,128]{1,2,0:T(8,128)(2,1)S(1)}, u32[]{:S(2)}) copy-start(bf16[4,128,128]{1,2,0:T(8,128)(2,1)S(1)} %squeeze.117) | copy-start | bytes 393220
  221.6 35.3 %collective-permute-start.5 = (bf16[1,1,128,512]{3,2,1,0:T(8,128)(2,1)S(1)}, bf16[1,1,128,512]{3,2,1,0:T(8,128)(2,1)}, u32[]{:S(2)}, u32[]{:S(2)}) collective-permute-start(bf16[1,1,128,512]{3,2,1,0:T(8,128)(2,1)S(1)} %copy.402), channel_id=1, source_target_pairs={{4,0},{8,4},{12,8},{5,1},{9,5},{13,9},{6,2},{10,6},{14,10},{7,3},{... | collective-permute-start | bytes 393224 | tf_op jit(solution)/shard_map/ppermute | solution.py:20
  223.7 33.2 %collective-permute-start.4 = (bf16[1,1,128,512]{3,2,1,0:T(8,128)(2,1)}, bf16[1,1,128,512]{3,2,1,0:T(8,128)(2,1)}, u32[]{:S(2)}, u32[]{:S(2)}) collective-permute-start(bf16[1,1,128,512]{3,2,1,0:T(8,128)(2,1)} %copy.401), channel_id=1, source_target_pairs={{0,4},{4,8},{8,12},{1,5},{5,9},{9,13},{2,6},{6,10},{10,14},{3,7},{... | collective-permute-start | bytes 393224 | tf_op jit(solution)/shard_map/ppermute | solution.py:18
  249.8 97.5 %reduce-scatter.19.cloned.1.call-start = ((), (), s32[]{:S(2)}) async-start(), calls=%async_computation.5 | async-start | bytes 655360
  287.2 9.7 %copy-start.78 = (bf16[4,128,128]{2,1,0:T(8,128)(2,1)S(1)}, bf16[4,128,128]{2,1,0:T(8,128)(2,1)}, u32[]{:S(2)}) copy-start(bf16[4,128,128]{2,1,0:T(8,128)(2,1)} %fusion.79) | copy-start | bytes 393220
  289.5 37.1 %collective-permute-start.7 = (bf16[1,1,128,512]{3,2,1,0:T(8,128)(2,1)}, bf16[1,1,128,512]{3,2,1,0:T(8,128)(2,1)}, u32[]{:S(2)}, u32[]{:S(2)}) collective-permute-start(bf16[1,1,128,512]{3,2,1,0:T(8,128)(2,1)} %copy.406), channel_id=1, source_target_pairs={{4,0},{8,4},{12,8},{5,1},{9,5},{13,9},{6,2},{10,6},{14,10},{7,3},{... | collective-permute-start | bytes 393224 | tf_op jit(solution)/shard_map/ppermute | solution.py:20
  291.5 35.1 %collective-permute-start.6 = (bf16[1,1,128,512]{3,2,1,0:T(8,128)(2,1)}, bf16[1,1,128,512]{3,2,1,0:T(8,128)(2,1)}, u32[]{:S(2)}, u32[]{:S(2)}) collective-permute-start(bf16[1,1,128,512]{3,2,1,0:T(8,128)(2,1)} %copy.405), channel_id=1, source_target_pairs={{0,4},{4,8},{8,12},{1,5},{5,9},{9,13},{2,6},{6,10},{10,14},{3,7},{... | collective-permute-start | bytes 393224 | tf_op jit(solution)/shard_map/ppermute | solution.py:18
  310.3 45.9 %reduce-scatter.21.cloned.1.call-start = ((), (), s32[]{:S(2)}) async-start(), calls=%async_computation.6 | async-start | bytes 655360
  325.9 55.0 %reduce-scatter.17.cloned.1.call-start = ((), (), s32[]{:S(2)}) async-start(), calls=%async_computation.4 | async-start | bytes 655360
  329.2 14.9 %copy-start.117 = (u32[32]{0:T(128)S(1)}, u32[32]{0:T(128)}, u32[]{:S(2)}) copy-start(u32[32]{0:T(128)} %constant.395) | copy-start | bytes 388
  330.2 93.8 %all-reduce.12.cloned.1.call-start = ((), (), s32[]{:S(2)}) async-start(), calls=%async_computation.8 | async-start | bytes 1212416 | tf_op jit(solution)/shard_map/psum | solution.py:167
  339.0 6.3 %collective-permute-start.9 = (bf16[12,512]{1,0:T(8,128)(2,1)S(1)}, bf16[12,512]{1,0:T(8,128)(2,1)S(1)}, u32[]{:S(2)}, u32[]{:S(2)}) collective-permute-start(bf16[12,512]{1,0:T(8,128)(2,1)S(1)} %slice.573), channel_id=1, source_target_pairs={{0,1},{1,2},{2,3},{4,5},{5,6},{6,7},{8,9},{9,10},{10,11},{12,13},{... | collective-permute-start | bytes 36872
  340.3 5.1 %collective-permute-start.8 = (bf16[12,512]{1,0:T(8,128)(2,1)S(1)}, bf16[12,512]{1,0:T(8,128)(2,1)S(1)}, u32[]{:S(2)}, u32[]{:S(2)}) collective-permute-start(bf16[12,512]{1,0:T(8,128)(2,1)S(1)} %slice.572), channel_id=1, source_target_pairs={{0,1},{1,2},{2,3},{4,5},{5,6},{6,7},{8,9},{9,10},{10,11},{12,13},{... | collective-permute-start | bytes 36872
  348.4 34.3 %copy-start.20 = (bf16[1,512,512]{2,1,0:T(8,128)(2,1)S(1)}, bf16[1,512,512]{2,1,0:T(8,128)(2,1)}, u32[]{:S(2)}) copy-start(bf16[1,512,512]{2,1,0:T(8,128)(2,1)} %copy-done.19) | copy-start | bytes 1572868
  348.4 34.3 %copy-start.66 = (f32[256,512]{1,0:T(8,128)S(1)}, f32[256,512]{1,0:T(8,128)}, u32[]{:S(2)}) copy-start(f32[256,512]{1,0:T(8,128)} %copy-done.64) | copy-start | bytes 1572868
  (114 other events, 213.2 us)
Sparse Core Ops, SparseCore 0:
  250.0 21.4 reduce-scatter.22
  310.4 21.4 reduce-scatter.18
  334.5 21.6 reduce-scatter.20
  359.2 21.6 reduce-scatter.16
  383.9 40.0 all-reduce.11
where the time goes:
time: 443 us; the launch traced here: 435 us
  local copies, waits for them, and re-layouts  196 us (44%)
  waiting for transfers between devices  71.1 us (16%)
  blocking collectives  54.5 us (12%)
  matrix products  44.2 us (10%)
  starting transfers between devices  31.5 us (7%)
  other arithmetic  20.9 us (5%)
  between operations  16.9 us (4%)
    reshape x52, local copies, waits for them, and re-layouts, grouped_taps(): window = window.reshape(-1, kernel.shape[1], kernel.shape[2])  52.9 us
    squeeze x18, local copies, waits for them, and re-layouts, grouped_taps(): kernel[tap_index]  42 us
    psum x1, waiting for transfers between devices, body(): lax.psum(jnp.stack([entry[0] for entry in shares]).astype(jnp.bfloat16),...  40.3 us
    unnamed x283, local copies, waits for them, and re-layouts  31.7 us
    unnamed x11, waiting for transfers between devices  30.8 us
    ppermute x4, starting transfers between devices, extended_2(): lax.ppermute(tail, axis, [(i, (i + 1) % count) for i in range(ends)])  21 us
    all_gather x2, blocking collectives, body(): lax.all_gather(weight_in[block_index], 'shard', axis=0, tiled=True)  17.9 us
    dot_general x36, matrix products, grouped_taps(): jnp.einsum(pattern, window, kernel[tap_index], preferred_element_type=jnp...  16.2 us
  transfers between devices with their start and end apart: 15, of which 3 were waited for; matrix products, arithmetic and copies ran while one was open for 38% of the time, Pallas kernels for 0%

commit v1 on v0

--- a/solution.py
+++ b/solution.py
@@ -164,9 +164,10 @@
         )
     shares = shares[::-1]
     totals = (
-        lax.psum(jnp.stack([entry[0] for entry in shares]).astype(jnp.bfloat16), "rows").astype(
-            jnp.float32
-        ),
+        jnp.sum(
+            lax.all_gather(jnp.stack([entry[0] for entry in shares]).astype(jnp.bfloat16), "rows"),
+            axis=0,
+        ).astype(jnp.float32),
         lax.psum(jnp.stack([entry[1] for entry in shares]).astype(jnp.bfloat16), "rows").astype(
             jnp.float32
         ),

time: 443 us -> 454 us (1.025)
  waiting for transfers between devices: 71.1 us -> 84.5 us
  local copies, waits for them, and re-layouts: 196 us -> 189 us
    all_gather x0 -> x1, waiting for transfers between devices: none -> 25.8 us  [body(): lax.all_gather(jnp.stack([entry[0] for entry in shares]).astype(jnp.bfloa...]
    unnamed x11 -> x10, waiting for transfers between devices: 30.8 us -> 22.3 us
    unnamed x283 -> x257, local copies, waits for them, and re-layouts: 31.7 us -> 28.6 us
  transfers between devices with their start and end apart: 15 -> 16, of which waited for: 3 -> 3; matrix products, arithmetic and copies ran while one was open for 38% -> 37% of each run, Pallas kernels for 0% -> 0%
where the time goes in v1:
time: 454 us; the launch traced here: 446 us
  local copies, waits for them, and re-layouts  189 us (42%)
  waiting for transfers between devices  84.5 us (19%)
  blocking collectives  54.5 us (12%)
  matrix products  44.2 us (10%)
  starting transfers between devices  31.6 us (7%)
  other arithmetic  25.1 us (6%)
  between operations  17.1 us (4%)
    reshape x52, local copies, waits for them, and re-layouts, grouped_taps(): window = window.reshape(-1, kernel.shape[1], kernel.shape[2])  52.9 us
    squeeze x18, local copies, waits for them, and re-layouts, grouped_taps(): kernel[tap_index]  42 us
    psum x1, waiting for transfers between devices, body(): lax.psum(jnp.stack([entry[1] for entry in shares]).astype(jnp.bfloat16),...  36.4 us
    unnamed x257, local copies, waits for them, and re-layouts  28.6 us
    all_gather x1, waiting for transfers between devices, body(): lax.all_gather(jnp.stack([entry[0] for entry in shares]).astype(jnp.bfloa...  25.8 us
    unnamed x10, waiting for transfers between devices  22.3 us
    ppermute x4, starting transfers between devices, extended_2(): lax.ppermute(tail, axis, [(i, (i + 1) % count) for i in range(ends)])  21 us
    all_gather x2, blocking collectives, body(): lax.all_gather(weight_in[block_index], 'shard', axis=0, tiled=True)  17.9 us
  transfers between devices with their start and end apart: 16, of which 3 were waited for; matrix products, arithmetic and copies ran while one was open for 37% of the time, Pallas kernels for 0%

profile of v1, /device:TPU:0, one launch (start us, length us, event | category | flops | bytes accessed | tf_op | source)
XLA Modules:
  0.0 445.9 jit_solution(1433716358149559118)
XLA Ops:
  8.9 8.6 %all-gather.1 = bf16[1,512,512]{2,1,0:T(8,128)(2,1)S(1)} all-gather(bf16[1,128,512]{2,1,0:T(8,128)(2,1)S(1)} %get-tuple-element.131), channel_id=3, replica_groups=mesh['groups'=2,'rows'=4,'shard'=4] {'shard'}, dimensions={1}, use_global_device_ids=true | all-gather | bytes 655360 | tf_op jit(solution)/shard_map/all_gather | solution.py:69
  20.6 5.2 %collective-permute-start = (bf16[1,1,128,512]{3,2,1,0:T(8,128)(2,1)}, bf16[1,1,128,512]{3,2,1,0:T(8,128)(2,1)}, u32[]{:S(2)}, u32[]{:S(2)}) collective-permute-start(bf16[1,1,128,512]{3,2,1,0:T(8,128)(2,1)} %get-tuple-element.129), channel_id=1, source_target_pairs={{0,4},{4,8},{8,12},{1,5},{5,9},{9,13},{2,6},{6,10},{10,14},{3,7},{... | collective-permute-start | bytes 393224 | tf_op jit(solution)/shard_map/ppermute | solution.py:18
  27.5 5.9 %all-gather = bf16[1,144,512]{2,0,1:T(2,128)(2,1)S(1)} all-gather(bf16[1,36,512]{2,0,1:T(2,128)(2,1)S(1)} %get-tuple-element.135), channel_id=2, replica_groups=mesh['groups'=2,'rows'=4,'shard'=4] {'shard'}, dimensions={1}, use_global_device_ids=true | all-gather | bytes 184320 | tf_op jit(solution)/shard_map/all_gather | solution.py:70
  36.6 6.0 %all-gather.3 = bf16[1,144,512]{2,0,1:T(2,128)(2,1)S(1)} all-gather(bf16[1,36,512]{2,0,1:T(2,128)(2,1)S(1)} %get-tuple-element.136), channel_id=5, replica_groups=mesh['groups'=2,'rows'=4,'shard'=4] {'shard'}, dimensions={1}, use_global_device_ids=true | all-gather | bytes 184320 | tf_op jit(solution)/shard_map/all_gather | solution.py:70
  45.9 9.3 %all-gather.4 = bf16[1,512,512]{2,1,0:T(8,128)(2,1)} all-gather(bf16[1,128,512]{2,1,0:T(8,128)(2,1)} %get-tuple-element.132), channel_id=6, replica_groups=mesh['groups'=2,'rows'=4,'shard'=4] {'shard'}, dimensions={1}, use_global_device_ids=true | all-gather | bytes 655360 | tf_op jit(solution)/shard_map/all_gather | solution.py:69
  55.2 4.4 broadcast_multiply_fusion.1
  59.6 9.0 %fusion.109 = (bf16[1,4,8,16,8,16]{3,2,5,4,1,0:T(8,128)(2,1)S(1)}, bf16[1,4,8,16,8,16]{3,2,5,4,1,0:T(8,128)(2,1)S(1)}, bf16[1,4,8,16,8,16]{3,2,5,4,1,0:T(8,128)(...) fusion(bf16[9,4,8,16,8,16]{3,2,5,4,1,0:T(8,128)(2,1)} %get-tupl, ...), kind=kLoop, calls=%fused_computation.285 | loop fusion | bytes 4718592 | tf_op jit(solution)/shard_map/slice | solution.py:54
  70.6 2.6 squeeze.99
  73.2 2.6 squeeze.100
  81.1 2.6 squeeze.103
  88.9 2.6 squeeze.106
  91.5 8.8 %all-gather.2 = bf16[1,512,512]{2,1,0:T(8,128)(2,1)} all-gather(bf16[1,128,512]{2,1,0:T(8,128)(2,1)} %get-tuple-element.133), channel_id=4, replica_groups=mesh['groups'=2,'rows'=4,'shard'=4] {'shard'}, dimensions={1}, use_global_device_ids=true | all-gather | bytes 655360 | tf_op jit(solution)/shard_map/all_gather | solution.py:71
  143.6 5.2 %collective-permute-start.2 = (bf16[1,1,128,512]{3,2,1,0:T(8,128)(2,1)}, bf16[1,1,128,512]{3,2,1,0:T(8,128)(2,1)}, u32[]{:S(2)}, u32[]{:S(2)}) collective-permute-start(bf16[1,1,128,512]{3,2,1,0:T(8,128)(2,1)} %get-tuple-element.125), channel_id=1, source_target_pairs={{0,4},{4,8},{8,12},{1,5},{5,9},{9,13},{2,6},{6,10},{10,14},{3,7},{... | collective-permute-start | bytes 393224 | tf_op jit(solution)/shard_map/ppermute | solution.py:18
  148.8 7.2 %all-gather.5 = bf16[1,512,512]{2,1,0:T(8,128)(2,1)} all-gather(bf16[1,128,512]{2,1,0:T(8,128)(2,1)S(1)} %copy-done.92), channel_id=7, replica_groups=mesh['groups'=2,'rows'=4,'shard'=4] {'shard'}, dimensions={1}, use_global_device_ids=true | all-gather | bytes 655360 | tf_op jit(solution)/shard_map/all_gather | solution.py:71
  156.0 2.6 squeeze.109
  169.0 2.8 squeeze.115
  186.2 2.7 convert_multiply_fusion
  223.6 5.2 %collective-permute-start.4 = (bf16[1,1,128,512]{3,2,1,0:T(8,128)(2,1)}, bf16[1,1,128,512]{3,2,1,0:T(8,128)(2,1)}, u32[]{:S(2)}, u32[]{:S(2)}) collective-permute-start(bf16[1,1,128,512]{3,2,1,0:T(8,128)(2,1)} %copy.389), channel_id=1, source_target_pairs={{0,4},{4,8},{8,12},{1,5},{5,9},{9,13},{2,6},{6,10},{10,14},{3,7},{... | collective-permute-start | bytes 393224 | tf_op jit(solution)/shard_map/ppermute | solution.py:18
  297.8 5.4 %collective-permute-start.6 = (bf16[1,1,128,512]{3,2,1,0:T(8,128)(2,1)}, bf16[1,1,128,512]{3,2,1,0:T(8,128)(2,1)}, u32[]{:S(2)}, u32[]{:S(2)}) collective-permute-start(bf16[1,1,128,512]{3,2,1,0:T(8,128)(2,1)} %copy.393), channel_id=1, source_target_pairs={{0,4},{4,8},{8,12},{1,5},{5,9},{9,13},{2,6},{6,10},{10,14},{3,7},{... | collective-permute-start | bytes 393224 | tf_op jit(solution)/shard_map/ppermute | solution.py:18
  326.8 8.6 %fusion.108 = (bf16[40,512]{1,0:T(8,128)(2,1)S(1)}, bf16[40,512]{1,0:T(8,128)(2,1)S(1)}) fusion(bf16[144,512]{1,0:T(8,128)(2,1)} %bitcast.72, bf16[144,512]{1,0:T(8,128)(2,1)S(1)} %bitcast.607), kind=kCustom, calls=%all-reduce-scatter.2 | all-reduce-scatter fusion | flops 163841 | bytes 377344
  336.8 3.7 collective-permute-start.8
  345.7 22.2 %reduce-scatter.17.cloned.1.call-done = bf16[128,512]{1,0:T(8,128)(2,1)} async-done(((bf16[512,512]{1,0:T(8,128)(2,1)}), bf16[128,512]{1,0:T(8,128)(2,1)}) %reduce-scatter.17.cloned.1.call-update) | async-done | bytes 131088
  370.9 36.4 %all-reduce.12.cloned.1.call-done = (bf16[2,36,512]{2,1,0:T(8,128)(2,1)}, bf16[2,128,512]{2,1,0:T(8,128)(2,1)}) async-done(((bf16[2,36,512]{2,1,0:T(8,128)(2,1)}, bf16[2,128,512]{2,1,0:T(8,128)(2,1)}), (bf16[2,36,512]{2,1,0:T(8,128)(2,1)}, bf16[2,128,512]{2,1,0:T(8,128)(2,1)})) %all-reduce.12.cloned.1.call-update) | async-done | bytes 335888 | tf_op jit(solution)/shard_map/psum | solution.py:171
  410.8 25.8 %all-gather.8.cloned.1.call-done = bf16[4,2,128,512]{3,2,1,0:T(8,128)(2,1)} async-done(((bf16[1,2,128,512]{3,2,1,0:T(8,128)(2,1)}), bf16[4,2,128,512]{3,2,1,0:T(8,128)(2,1)}) %all-gather.8.cloned.1.call-update) | async-done | bytes 1048592 | tf_op jit(solution)/shard_map/all_gather | solution.py:168
  (557 shorter events, 233.2 us)
Async XLA Ops:
  7.2 10.3 %copy-start.97 = (bf16[1,2,128,512]{3,2,1,0:T(8,128)(2,1)S(1)}, bf16[1,2,128,512]{3,2,1,0:T(8,128)(2,1)}, u32[]{:S(2)}) copy-start(bf16[1,2,128,512]{3,2,1,0:T(8,128)(2,1)} %param.13) | copy-start | bytes 786436
  7.2 335.6 %reduce-scatter.15.cloned.1.call-start = ((), (), s32[]{:S(2)}) async-start(), calls=%async_computation.6 | async-start | bytes 655360 | tf_op jit(solution)/shard_map/reduce_scatter | solution.py:160
  18.6 14.8 %copy-start = (bf16[256,512]{1,0:T(8,128)(2,1)}, bf16[256,512]{1,0:T(8,128)(2,1)S(1)}, u32[]{:S(2)}) copy-start(bf16[256,512]{1,0:T(8,128)(2,1)S(1)} %get-tuple-element.139) | copy-start | bytes 786436
  18.6 8.8 %copy-start.93 = (bf16[2,36,512]{2,0,1:T(2,128)(2,1)S(1)}, bf16[2,36,512]{2,0,1:T(2,128)(2,1)}, u32[]{:S(2)}) copy-start(bf16[2,36,512]{2,0,1:T(2,128)(2,1)} %param.16) | copy-start | bytes 221188
  19.3 81.0 %collective-permute-start.1 = (bf16[1,1,128,512]{3,2,1,0:T(8,128)(2,1)}, bf16[1,1,128,512]{3,2,1,0:T(8,128)(2,1)}, u32[]{:S(2)}, u32[]{:S(2)}) collective-permute-start(bf16[1,1,128,512]{3,2,1,0:T(8,128)(2,1)} %get-tuple-element.130), channel_id=1, source_target_pairs={{4,0},{8,4},{12,8},{5,1},{9,5},{13,9},{6,2},{10,6},{14,10},{7,3},{... | collective-permute-start | bytes 393224 | tf_op jit(solution)/shard_map/ppermute | solution.py:20
  20.6 79.7 %collective-permute-start = (bf16[1,1,128,512]{3,2,1,0:T(8,128)(2,1)}, bf16[1,1,128,512]{3,2,1,0:T(8,128)(2,1)}, u32[]{:S(2)}, u32[]{:S(2)}) collective-permute-start(bf16[1,1,128,512]{3,2,1,0:T(8,128)(2,1)} %get-tuple-element.129), channel_id=1, source_target_pairs={{0,4},{4,8},{8,12},{1,5},{5,9},{9,13},{2,6},{6,10},{10,14},{3,7},{... | collective-permute-start | bytes 393224 | tf_op jit(solution)/shard_map/ppermute | solution.py:18
  88.9 11.5 %copy-start.1 = (bf16[256,512]{1,0:T(8,128)(2,1)S(1)}, bf16[256,512]{1,0:T(8,128)(2,1)}, u32[]{:S(2)}) copy-start(bf16[256,512]{1,0:T(8,128)(2,1)} %copy-done) | copy-start | bytes 786436
  142.3 33.0 %collective-permute-start.3 = (bf16[1,1,128,512]{3,2,1,0:T(8,128)(2,1)}, bf16[1,1,128,512]{3,2,1,0:T(8,128)(2,1)}, u32[]{:S(2)}, u32[]{:S(2)}) collective-permute-start(bf16[1,1,128,512]{3,2,1,0:T(8,128)(2,1)} %get-tuple-element.126), channel_id=1, source_target_pairs={{4,0},{8,4},{12,8},{5,1},{9,5},{13,9},{6,2},{10,6},{14,10},{7,3},{... | collective-permute-start | bytes 393224 | tf_op jit(solution)/shard_map/ppermute | solution.py:20
  143.6 31.8 %collective-permute-start.2 = (bf16[1,1,128,512]{3,2,1,0:T(8,128)(2,1)}, bf16[1,1,128,512]{3,2,1,0:T(8,128)(2,1)}, u32[]{:S(2)}, u32[]{:S(2)}) collective-permute-start(bf16[1,1,128,512]{3,2,1,0:T(8,128)(2,1)} %get-tuple-element.125), channel_id=1, source_target_pairs={{0,4},{4,8},{8,12},{1,5},{5,9},{9,13},{2,6},{6,10},{10,14},{3,7},{... | collective-permute-start | bytes 393224 | tf_op jit(solution)/shard_map/ppermute | solution.py:18
  173.8 10.5 %copy-start.48 = (bf16[4,128,128]{1,2,0:T(8,128)(2,1)}, bf16[4,128,128]{1,2,0:T(8,128)(2,1)S(1)}, u32[]{:S(2)}) copy-start(bf16[4,128,128]{1,2,0:T(8,128)(2,1)S(1)} %squeeze.117) | copy-start | bytes 393220
  221.6 35.3 %collective-permute-start.5 = (bf16[1,1,128,512]{3,2,1,0:T(8,128)(2,1)S(1)}, bf16[1,1,128,512]{3,2,1,0:T(8,128)(2,1)}, u32[]{:S(2)}, u32[]{:S(2)}) collective-permute-start(bf16[1,1,128,512]{3,2,1,0:T(8,128)(2,1)S(1)} %copy.390), channel_id=1, source_target_pairs={{4,0},{8,4},{12,8},{5,1},{9,5},{13,9},{6,2},{10,6},{14,10},{7,3},{... | collective-permute-start | bytes 393224 | tf_op jit(solution)/shard_map/ppermute | solution.py:20
  223.6 33.2 %collective-permute-start.4 = (bf16[1,1,128,512]{3,2,1,0:T(8,128)(2,1)}, bf16[1,1,128,512]{3,2,1,0:T(8,128)(2,1)}, u32[]{:S(2)}, u32[]{:S(2)}) collective-permute-start(bf16[1,1,128,512]{3,2,1,0:T(8,128)(2,1)} %copy.389), channel_id=1, source_target_pairs={{0,4},{4,8},{8,12},{1,5},{5,9},{9,13},{2,6},{6,10},{10,14},{3,7},{... | collective-permute-start | bytes 393224 | tf_op jit(solution)/shard_map/ppermute | solution.py:18
  249.8 93.0 %reduce-scatter.13.cloned.1.call-start = ((), (), s32[]{:S(2)}) async-start(), calls=%async_computation.5 | async-start | bytes 655360 | tf_op jit(solution)/shard_map/reduce_scatter | solution.py:160
  292.6 52.0 %reduce-scatter.19.cloned.1.call-start = ((), (), s32[]{:S(2)}) async-start(), calls=%async_computation.8 | async-start | bytes 655360
  295.7 27.4 %collective-permute-start.7 = (bf16[1,1,128,512]{3,2,1,0:T(8,128)(2,1)}, bf16[1,1,128,512]{3,2,1,0:T(8,128)(2,1)}, u32[]{:S(2)}, u32[]{:S(2)}) collective-permute-start(bf16[1,1,128,512]{3,2,1,0:T(8,128)(2,1)} %copy.394), channel_id=1, source_target_pairs={{4,0},{8,4},{12,8},{5,1},{9,5},{13,9},{6,2},{10,6},{14,10},{7,3},{... | collective-permute-start | bytes 393224 | tf_op jit(solution)/shard_map/ppermute | solution.py:20
  297.8 25.3 %collective-permute-start.6 = (bf16[1,1,128,512]{3,2,1,0:T(8,128)(2,1)}, bf16[1,1,128,512]{3,2,1,0:T(8,128)(2,1)}, u32[]{:S(2)}, u32[]{:S(2)}) collective-permute-start(bf16[1,1,128,512]{3,2,1,0:T(8,128)(2,1)} %copy.393), channel_id=1, source_target_pairs={{0,4},{4,8},{8,12},{1,5},{5,9},{9,13},{2,6},{6,10},{10,14},{3,7},{... | collective-permute-start | bytes 393224 | tf_op jit(solution)/shard_map/ppermute | solution.py:18
  321.2 46.7 %reduce-scatter.17.cloned.1.call-start = ((), (), s32[]{:S(2)}) async-start(), calls=%async_computation.7 | async-start | bytes 655360
  325.6 14.9 %copy-start.106 = (u32[32]{0:T(128)S(1)}, u32[32]{0:T(128)}, u32[]{:S(2)}) copy-start(u32[32]{0:T(128)} %constant.397) | copy-start | bytes 388
  326.7 80.6 %all-reduce.12.cloned.1.call-start = ((), (), s32[]{:S(2)}) async-start(), calls=%async_computation.9 | async-start | bytes 688128 | tf_op jit(solution)/shard_map/psum | solution.py:171
  335.4 6.3 %collective-permute-start.9 = (bf16[12,512]{1,0:T(8,128)(2,1)S(1)}, bf16[12,512]{1,0:T(8,128)(2,1)S(1)}, u32[]{:S(2)}, u32[]{:S(2)}) collective-permute-start(bf16[12,512]{1,0:T(8,128)(2,1)S(1)} %slice.573), channel_id=1, source_target_pairs={{0,1},{1,2},{2,3},{4,5},{5,6},{6,7},{8,9},{9,10},{10,11},{12,13},{... | collective-permute-start | bytes 36872
  336.8 5.2 %collective-permute-start.8 = (bf16[12,512]{1,0:T(8,128)(2,1)S(1)}, bf16[12,512]{1,0:T(8,128)(2,1)S(1)}, u32[]{:S(2)}, u32[]{:S(2)}) collective-permute-start(bf16[12,512]{1,0:T(8,128)(2,1)S(1)} %slice.572), channel_id=1, source_target_pairs={{0,1},{1,2},{2,3},{4,5},{5,6},{6,7},{8,9},{9,10},{10,11},{12,13},{... | collective-permute-start | bytes 36872
  344.5 25.3 %copy-start.20 = (bf16[1,512,512]{2,1,0:T(8,128)(2,1)S(1)}, bf16[1,512,512]{2,1,0:T(8,128)(2,1)}, u32[]{:S(2)}) copy-start(bf16[1,512,512]{2,1,0:T(8,128)(2,1)} %copy-done.19) | copy-start | bytes 1572868
  344.5 25.3 %copy-start.66 = (f32[256,512]{1,0:T(8,128)S(1)}, f32[256,512]{1,0:T(8,128)}, u32[]{:S(2)}) copy-start(f32[256,512]{1,0:T(8,128)} %copy-done.64) | copy-start | bytes 1572868
  344.5 92.0 %all-gather.8.cloned.1.call-start = ((), (), s32[]{:S(2)}) async-start(), calls=%async_computation.4 | async-start | bytes 1310720 | tf_op jit(solution)/shard_map/all_gather | solution.py:168
  (104 other events, 195.9 us)
Sparse Core Ops, SparseCore 0:
  250.0 21.4 reduce-scatter.14
  292.7 21.4 reduce-scatter.12
  321.4 21.4 reduce-scatter.18
  346.0 21.8 reduce-scatter.16
  370.7 36.4 all-reduce.11
  408.7 27.7 all-gather.7
